TPU v7x, 128 devices: a whole 4x4x4 slice. The times are simulated.
128 devices in a mesh: grp: 4 (over x_hi, core), tile: 32 (over x_lo, y, z).
Axes of the slice: x: 4 (x_hi: 2, x_lo: 2; x = x_hi * 2 + x_lo), y: 4, z: 4, core: 2. Of those that a mesh axis runs over, the one named last changes fastest.
Arguments:
- start_field: float32 [512, 512, 512], P('grp', 'tile'), may hold values from -4 to 4
- class_ids: int32 [512, 512], P('tile'), may hold values from 0 to 7
- run_levels: int32 [512, 8], replicated, may hold values from 0 to 7
- steepness: float32 [512], replicated, may hold values from 0.1 to 1
- step_pick: int32 [512], replicated, may hold values from 1 to 4
- input_layer: float32 [69, 2048], replicated, may hold values from -2 to 2
- output_layer: bfloat16 [2048, 262144], P(None, ('grp', 'tile')), may hold values from -0.125 to 0.125
- output_bias: float32 [262144], P(('grp', 'tile')), may hold values from -1.5 to 1.5
Outputs:
- misfit: bfloat16 [512, 262144], P(None, ('grp', 'tile'))
- output_next: bfloat16 [2048, 262144], P(None, ('grp', 'tile'))
- bias_next: float32 [262144], P(('grp', 'tile'))
- input_next: float32 [69, 2048], replicated
All inputs are finite; a program needn't handle non-finite values.
Results may differ from a plain program's by a relative error of at most 0.0029.
The roundings to bfloat16 on the way count: a program that leaves them out, or rounds other values in their place, can miss the bound.
Values sent between devices are 32-bit elements; how exact they have to be, the bound alone decides.
A program may use at most 128 MiB of HBM per device.

v0:
```python
import jax
import jax.numpy as jnp
from jax import lax
from jax.sharding import Mesh
from jax.sharding import PartitionSpec as P

STEPS = 4
LEVELS = 8
GRP = ("grp_0", "grp_1")
GRP_TILE = ("grp_0", "grp_1", "tile")


def with_halo(value, sides, width):
    for axis, dim in sides:
        size, length = (lax.axis_size(axis), value.shape[dim])
        up = [(i, (i + 1) % size) for i in range(size - 1)]
        down = [(j, i) for i, j in up]
        last = lax.slice_in_dim(value, length - width, length, axis=dim)
        initial = lax.slice_in_dim(value, 0, width, axis=dim)
        before = lax.ppermute(last, axis, up)
        after = lax.ppermute(initial, axis, down)
        value = jnp.concatenate([before, value, after], axis=dim)
    return value


def in_blocks(value, dim, length):
    shape = value.shape
    tiles = value.reshape(*shape[:dim], length, shape[dim] // length, *shape[dim + 1 :])
    return jnp.moveaxis(tiles, dim, 0)


def in_order(tiles, dim):
    tiles = jnp.moveaxis(tiles, 0, dim)
    shape = tiles.shape
    return tiles.reshape(*shape[:dim], shape[dim] * shape[dim + 1], *shape[dim + 2 :])


def turned_blocks(tiles, axes, order):
    inside = tiles.shape[1:]
    out = tiles.reshape(*(lax.axis_size(a) for a in axes), *inside)
    for k in order:
        out = lax.all_to_all(out, axes[k], k, k, tiled=True)
    return out.reshape(-1, *inside)


def core_and_chips(value, groups, order, split_dim, concat_dim):
    length = lax.axis_size(groups[0]) * lax.axis_size(groups[1])
    tiles = in_blocks(value, split_dim, length)
    return in_order(turned_blocks(tiles, groups, order), concat_dim)


def coefficients(run_levels, class_ids):
    table = 0.03 * jnp.exp(run_levels.astype(jnp.float32) * jnp.log(jnp.float32(1.35)))
    kappa = jnp.zeros((run_levels.shape[0],) + class_ids.shape, jnp.float32)
    for klass in range(run_levels.shape[1]):
        picked = jnp.where(class_ids == klass, 1.0, 0.0).astype(jnp.float32)
        kappa = kappa + picked[None] * table[:, klass][:, None, None]
    return kappa


def advance(field, kappa, steep):
    ratio = field * field
    spread = kappa * (1.0 + steep * ratio) / (1.0 + ratio)
    fpad = jnp.pad(field, ((0, 0), (0, 0), (1, 1)))
    spad = jnp.pad(spread, ((0, 0), (0, 0), (1, 1)))
    centre = field[:, 1:-1]
    middle = spread[:, 1:-1]
    total = centre + 0.5 * (middle + spread[:, :-2]) * (field[:, :-2] - centre)
    total = total + 0.5 * (middle + spread[:, 2:]) * (field[:, 2:] - centre)
    total = total + 0.5 * (middle + spad[:, 1:-1, :-2]) * (fpad[:, 1:-1, :-2] - centre)
    total = total + 0.5 * (middle + spad[:, 1:-1, 2:]) * (fpad[:, 1:-1, 2:] - centre)
    return total


def features(run_levels, step_pick, steepness):
    count = run_levels.shape[0]
    onehot = (run_levels[:, :, None] == jnp.arange(LEVELS, dtype=jnp.int32)[None, None, :]).astype(
        jnp.float32
    )
    onehot = onehot.reshape(count, -1)
    moment = (step_pick[:, None] == jnp.arange(1, STEPS + 1, dtype=jnp.int32)[None, :]).astype(
        jnp.float32
    )
    return jnp.concatenate([onehot, moment, steepness[:, None]], axis=1)


def dsilu(pre):
    logistic = jax.nn.sigmoid(pre)
    return logistic * (1.0 + pre * (1.0 - logistic))


def on_device(
    start_field, class_ids, run_levels, steepness, step_pick, input_layer, output_layer, output_bias
):
    local_runs, rows, columns = start_field.shape
    first_run = lax.axis_index(GRP) * local_runs
    levels_here = lax.dynamic_slice_in_dim(run_levels, first_run, local_runs, 0)
    steep = lax.dynamic_slice_in_dim(steepness, first_run, local_runs, 0)[:, None, None]
    pick_here = lax.dynamic_slice_in_dim(step_pick, first_run, local_runs, 0)[:, None, None]
    snapshot = jnp.zeros_like(start_field)
    class_wide = with_halo(class_ids + 1, (("tile", 0),), STEPS)
    kappa_wide = coefficients(levels_here, class_wide - 1)
    wide = with_halo(start_field, (("tile", 1),), STEPS)
    first_row = lax.axis_index("tile") * rows - STEPS
    total_rows = rows * lax.axis_size("tile")
    span = kappa_wide.shape[1]
    for step in range(STEPS):
        margin = STEPS - step - 1
        kappa_now = kappa_wide[:, step : span - step]
        wide = advance(wide, kappa_now, steep)
        row_ids = first_row + step + 1 + jnp.arange(wide.shape[1], dtype=jnp.int32)
        inside = (row_ids >= 0) & (row_ids < total_rows)
        wide = jnp.where(inside[None, :, None], wide, 0.0)
        snapshot = jnp.where(pick_here == step + 1, wide[:, margin : margin + rows], snapshot)
    flat = snapshot.reshape(local_runs, rows * columns)
    target = core_and_chips(flat, ("grp_0", "grp_1"), (0, 1), 1, 0)
    runs_total = target.shape[0]
    feats = features(run_levels, step_pick, steepness)
    pre = jnp.dot(feats, input_layer, precision=lax.Precision.HIGHEST)
    hidden = jax.nn.silu(pre).astype(jnp.bfloat16)
    error = (
        jnp.dot(hidden, output_layer, preferred_element_type=jnp.float32)
        + output_bias[None, :]
        - target
    )
    slope = (error * (2.0 / runs_total)).astype(jnp.bfloat16)
    grad = lax.dot_general(
        hidden, slope, (((0,), (0,)), ((), ())), preferred_element_type=jnp.float32
    )
    output_next = (output_layer.astype(jnp.float32) - 0.5 * grad).astype(jnp.bfloat16)
    bias_next = output_bias - 0.5 * jnp.sum(slope.astype(jnp.float32), axis=0)
    gain_slope = dsilu(pre)
    partial_back = lax.dot_general(
        slope, output_layer, (((1,), (1,)), ((), ())), preferred_element_type=jnp.float32
    )
    back = lax.psum(partial_back, GRP_TILE)
    grad_in = lax.dot_general(
        feats, back * gain_slope, (((0,), (0,)), ((), ())), precision=lax.Precision.HIGHEST
    )
    input_next = input_layer - 2.0 * grad_in
    return (error.astype(jnp.bfloat16), output_next, bias_next, input_next)


def solution(mesh):
    split = Mesh(mesh.devices.reshape(2, 2, mesh.shape["tile"]), ("grp_0", "grp_1", "tile"))
    return jax.shard_map(
        on_device,
        mesh=split,
        in_specs=(
            P(GRP, "tile", None),
            P("tile", None),
            P(),
            P(),
            P(),
            P(),
            P(None, GRP_TILE),
            P(GRP_TILE),
        ),
        out_specs=(P(None, GRP_TILE), P(None, GRP_TILE), P(GRP_TILE), P()),
        check_vma=False,
    )
```

profile of v0, /device:TPU:1, one launch (start us, length us, event | category | flops | bytes accessed | tf_op | source)
XLA Modules:
  0.0 393.0 jit_solution(14505002223111617005)
XLA Ops:
  7.2 0.0 copy-start.22
  7.2 0.8 broadcast_add_fusion
  8.0 4.4 %collective-permute-start.2 = (s32[4,512]{1,0:T(4,128)S(1)}, s32[4,512]{1,0:T(4,128)S(1)}, u32[]{:S(2)}, u32[]{:S(2)}) collective-permute-start(s32[4,512]{1,0:T(4,128)S(1)} %get-tuple-element.24), channel_id=1, source_target_pairs={{0,1},{1,2},{2,3},{3,4},{4,5},{5,6},{6,7},{7,8},{8,9},{9,10},{10,1... | collective-permute-start | bytes 24584 | tf_op jit(solution)/shard_map/ppermute | solution.py:20
  12.3 1.3 collective-permute-start.3
  13.6 2.7 fusion.96
  16.4 0.3 copy.34
  16.7 4.2 %collective-permute-start = (f32[128,4,512]{2,0,1:T(8,128)S(1)}, f32[128,4,512]{2,0,1:T(8,128)S(1)}, u32[]{:S(2)}, u32[]{:S(2)}) collective-permute-start(f32[128,4,512]{2,0,1:T(8,128)S(1)} %copy.34), channel_id=1, source_target_pairs={{0,1},{1,2},{2,3},{3,4},{4,5},{5,6},{6,7},{7,8},{8,9},{9,10},{10,1... | collective-permute-start | bytes 3145736 | tf_op jit(solution)/shard_map/ppermute | solution.py:20
  21.0 1.3 copy.35
  22.3 1.3 collective-permute-start.1
  23.6 0.0 copy-start.24
  23.7 0.6 compare_and_fusion.3
  24.3 0.6 compare_and_fusion
  24.8 0.6 compare_and_fusion.1
  25.4 1.3 broadcast_compare_fusion.3
  26.7 0.6 broadcast_compare_fusion.2
  27.3 0.6 compare_and_fusion.2
  27.8 5.3 %copy.29 = f32[128,16,512]{0,2,1:T(8,128)} copy(f32[128,16,512]{2,1,0:T(8,128)} %param.8) | data formatting | bytes 8388608 | tf_op args[0]
  33.1 0.8 dynamic_slice.11
  33.9 0.0 collective-permute-done.2
  33.9 0.0 collective-permute-done.3
  33.9 0.0 copy-start.8
  34.0 0.0 copy-start.10
  34.0 0.0 copy-start.12
  34.0 0.0 copy-start.14
  34.0 0.0 copy-start.16
  34.0 0.0 copy-start.18
  34.0 0.0 copy-start.20
  34.0 14.8 %multiply_add_fusion = f32[128,24,512]{0,2,1:T(8,128)} fusion(f32[128]{0:T(128)S(1)} %get-tuple-element.27, f32[24,512]{1,0:T(8,128)S(1)} %get-tuple-element.23, f32[128]{0:T(128)S(1)} %get-tuple-element.28, f32[24,512]{1,0:T(8,128)S(1)} %get-tuple-element.22, f32[128]{0:T(128)S(1)} %get-tuple-element.29, f32[24,512]{1,0:T(8,128)S(1)} %get-tuple-element.21, ...), kind=kLoop, calls=%fused_computation.3 | loop fusion | flops 23592960 | bytes 6688768 | tf_op jit(solution)/shard_map/add | solution.py:57
  48.8 0.0 copy-done.24
  49.0 0.0 collective-permute-done
  49.0 0.3 copy.28
  49.3 0.0 collective-permute-done.1
  49.3 1.5 copy.30
  50.9 0.0 copy-start.3
  50.9 1.0 copy-done.3
  51.9 0.0 copy-start.25
  52.0 2.7 pad_maximum_fusion
  54.7 0.6 copy-done.2
  55.4 15.7 %add_divide_fusion = f32[128,24,512]{0,2,1:T(8,128)S(1)} fusion(f32[128]{0:T(128)S(1)} %dynamic_slice.11, f32[128,4,512]{0,2,1:T(8,128)} %copy-done.3, f32[128,16,512]{0,2,1:T(8,128)S(1)} %copy-done.2, f32[128,4,512]{0,2,1:T(8,128)S(1)} %copy.28, f32[128]{0:T(128)S(1)} %copy-done.25, f32[24,512]{1,0:T(8,128)S(1)} %copy-done.9, f32[128]{0:T(128)S(1)} %copy-done.27, ...), kind=kLoop, calls=%fused_computation.2 | loop fusion | flops 36175872 | bytes 12980736 | tf_op jit(solution)/shard_map/div | solution.py:63
  71.1 11.3 %fusion.11 = (f32[128,22,512]{0,2,1:T(8,128)}, f32[128,22,512]{0,2,1:T(8,128)S(1)}) fusion(f32[128,24,512]{0,2,1:T(8,128)} %multiply_add_fusion, f32[128]{0:T(128)S(1)} %dynamic_slice.11, f32[128,24,512]{0,2,1:T(8,128)S(1)} %pad_maximum_fusion, f32[128,24,512]{0,2,1:T(8,128)S(1)} %add_divide_fusion, pred[22]{0:T(512)(128)(4,1)} %compare_and_fusion), kind=kLoop, calls=%fused_computation.20 | loop fusion | flops 38928384 | bytes 64487960 | tf_op jit(solution)/shard_map/div | solution.py:63
  82.4 16.6 %fusion.29 = (f32[128,20,512]{0,2,1:T(8,128)S(1)}, f32[128,20,512]{0,2,1:T(8,128)S(1)}) fusion(f32[128,24,512]{0,2,1:T(8,128)} %multiply_add_fusion, f32[128]{0:T(128)S(1)} %dynamic_slice.11, f32[128,22,512]{0,2,1:T(8,128)S(1)} %get-tuple-element.11, f32[128,22,512]{0,2,1:T(8,128)} %get-tuple-element.10, pred[20]{0:T(512)(128)(4,1)S(1)} %copy-done.46), kind=kLoop, calls=%fused_computation.47 | loop fusion | flops 35389440 | bytes 58721280 | tf_op jit(solution)/shard_map/div | solution.py:63
  99.1 10.9 %fusion.47 = (f32[128,18,512]{0,2,1:T(8,128)}, f32[128,18,512]{0,2,1:T(8,128)}) fusion(f32[128,24,512]{0,2,1:T(8,128)} %multiply_add_fusion, f32[128]{0:T(128)S(1)} %dynamic_slice.11, f32[128,20,512]{0,2,1:T(8,128)S(1)} %get-tuple-element.9, f32[128,20,512]{0,2,1:T(8,128)S(1)} %get-tuple-element.8, pred[18]{0:T(512)(128)(4,1)S(1)} %copy-done.45), kind=kLoop, calls=%fused_computation.74 | loop fusion | flops 31850496 | bytes 52954112 | tf_op jit(solution)/shard_map/div | solution.py:63
  110.0 21.7 %fusion.60 = f32[128,16,512]{0,2,1:T(8,128)} fusion(f32[128,18,512]{0,2,1:T(8,128)} %get-tuple-element.6, f32[128,18,512]{0,2,1:T(8,128)} %get-tuple-element.7, f32[128,22,512]{0,2,1:T(8,128)} %copy-done, f32[128,20,512]{0,2,1:T(8,128)} %copy-done.1, pred[16]{0:T(512)(128)(4,1)S(1)} %copy-done.44, pred[128]{0:T(512)(128)(4,1)S(1)} %copy-done.43, ...), kind=kLoop, calls=%fused_computation.95 | loop fusion | flops 26214400 | bytes 47186448 | tf_op jit(solution)/shard_map/jit(_where)/select_n | solution.py:114
  131.7 5.6 %copy.31 = f32[4,128,2048]{2,1,0:T(8,128)} copy(f32[4,128,2048]{1,2,0:T(8,128)} %bitcast.30) | data formatting | bytes 8388608 | tf_op jit(solution)/shard_map/transpose | solution.py:29
  137.3 5.8 %all-to-all-start = ((f32[2,2,128,2048]{3,2,1,0:T(8,128)}), f32[2,2,128,2048]{3,2,1,0:T(8,128)}, u32[]{:S(2)}, u32[]{:S(2)}) async-start(f32[2,2,128,2048]{3,2,1,0:T(8,128)} %bitcast.31), calls=%async_computation | async-start | bytes 8388608 | tf_op jit(solution)/shard_map/all_to_all | solution.py:42
  143.0 0.0 all-reduce.10.cloned.1.call-start
  143.1 0.1 eq.141
  143.2 0.1 compare_convert_fusion
  143.3 0.1 fusion.87
  143.4 5.1 %fusion.88 = f32[512,2048]{1,0:T(8,128)} fusion(f32[69,2048]{1,0:T(8,128)S(1)} %copy-done.5, f32[512,1]{0,1:T(1,128)S(1)} %bitcast.32, f32[512,4]{0,1:T(4,128)S(1)} %compare_convert_fusion, f32[512,64]{0,1:T(8,128)S(1)} %fusion.87), kind=kOutput, calls=%fused_computation.131 | convolution fusion | flops 868291584 | bytes 4900864 | tf_op jit(solution)/shard_map/dot_general | solution.py:119
  148.5 42.2 %all-to-all-done = f32[2,2,128,2048]{3,2,1,0:T(8,128)} async-done(((f32[2,2,128,2048]{3,2,1,0:T(8,128)}), f32[2,2,128,2048]{3,2,1,0:T(8,128)}, u32[]{:S(2)}, u32[]{:S(2)}) %all-to-all-start) | async-done | bytes 4194336 | tf_op jit(solution)/shard_map/all_to_all | solution.py:42
  190.6 2.6 copy.32
  193.2 0.0 slice-start.1
  193.3 9.2 %all_to_all.10 = f32[2,2,128,2048]{3,2,0,1:T(8,128)S(1)} all-to-all(f32[2,2,128,2048]{3,2,0,1:T(8,128)S(1)} %copy.32), channel_id=1, replica_groups=mesh['grp_0'=2,'grp_1'=2,'tile'=32] {'grp_1'}, dimensions={1} | all-to-all | bytes 8388608 | tf_op jit(solution)/shard_map/all_to_all | solution.py:42
  202.5 0.5 copy.33
  203.0 1.7 copy-done.4
  204.7 6.1 %convert_reduce_fusion = (f32[2048]{0:T(1024)S(1)}, bf16[512,2048]{1,0:T(8,128)(2,1)}, f32[512,2048]{1,0:T(8,128)S(1)}) fusion(f32[2,2,128,2048]{3,2,1,0:T(8,128)S(1)} %copy.33, f32[2048]{0:T(1024)S(1)} %copy-done.23, bf16[2048,2048]{1,0:T(8,128)(2,1)S(1)} %bitcast.35, f32[512,2048]{1,0:T(8,128)S(1)} %copy-done.4), kind=kOutput, calls=%fused_computation.121 | convolution fusion | flops 4307548160 | bytes 23085056 | tf_op jit(solution)/shard_map/dot_general | solution.py:122
  210.7 2.1 copy-done.47
  212.8 6.2 %fusion.92 = f32[512,2048]{1,0:T(8,128)} fusion(bf16[2048,2048]{1,0:T(8,128)(2,1)S(1)} %bitcast.35, f32[512,2048]{1,0:T(8,128)S(1)} %get-tuple-element.37), kind=kOutput, calls=%fused_computation.165 | convolution fusion | flops 4297064448 | bytes 16777216 | tf_op jit(solution)/shard_map/dot_general | solution.py:133
  219.0 0.0 all-reduce.10.cloned.1.call-update
  219.0 0.6 multiply_subtract_fusion
  219.6 14.6 %subtract_convert_fusion = bf16[2048,2048]{1,0:T(8,128)(2,1)} fusion(bf16[2048,2048]{1,0:T(8,128)(2,1)} %param.14, f32[512,2048]{1,0:T(8,128)} %copy-done.47, f32[512,2048]{1,0:T(8,128)} %fusion.88), kind=kOutput, calls=%fused_computation | convolution fusion | flops 4319084544 | bytes 25165824 | tf_op jit(solution)/shard_map/dot_general | solution.py:127
  234.2 143.7 %all-reduce.10.cloned.1.call-done = f32[512,2048]{1,0:T(8,128)} async-done(((f32[512,2048]{1,0:T(8,128)}), f32[512,2048]{1,0:T(8,128)}) %all-reduce.10.cloned.1.call-update) | async-done | bytes 4194320 | tf_op jit(solution)/shard_map/psum | solution.py:136
  377.9 8.2 %fusion.83 = f32[69,2048]{1,0:T(8,128)} fusion(f32[69,2048]{1,0:T(8,128)S(1)} %copy-done.5, f32[512,2048]{1,0:T(8,128)} %all-reduce.10.cloned.1.call-done, f32[512,2048]{1,0:T(8,128)} %fusion.88, f32[512,1]{0,1:T(1,128)S(1)} %bitcast.33, f32[512,4]{0,1:T(4,128)S(1)} %compare_convert_fusion, f32[512,64]{0,1:T(8,128)S(1)} %fusion.87), kind=kOutput, calls=%fused_computation.126 | convolution fusion | flops 876962816 | bytes 9660416 | tf_op jit(solution)/shard_map/dot_general | solution.py:137
  (91 shorter events, 0.3 us)
Async XLA Ops:
  7.2 16.4 %copy-start.22 = (s32[512,8]{0,1:T(8,128)S(1)}, s32[512,8]{0,1:T(8,128)}, u32[]{:S(2)}) copy-start(s32[512,8]{0,1:T(8,128)} %param.10) | copy-start | bytes 49156
  8.0 25.9 %collective-permute-start.2 = (s32[4,512]{1,0:T(4,128)S(1)}, s32[4,512]{1,0:T(4,128)S(1)}, u32[]{:S(2)}, u32[]{:S(2)}) collective-permute-start(s32[4,512]{1,0:T(4,128)S(1)} %get-tuple-element.24), channel_id=1, source_target_pairs={{0,1},{1,2},{2,3},{3,4},{4,5},{5,6},{6,7},{7,8},{8,9},{9,10},{10,1... | collective-permute-start | bytes 24584 | tf_op jit(solution)/shard_map/ppermute | solution.py:20
  12.3 21.6 %collective-permute-start.3 = (s32[4,512]{1,0:T(4,128)S(1)}, s32[4,512]{1,0:T(4,128)S(1)}, u32[]{:S(2)}, u32[]{:S(2)}) collective-permute-start(s32[4,512]{1,0:T(4,128)S(1)} %get-tuple-element.25), channel_id=1, source_target_pairs={{1,0},{2,1},{3,2},{4,3},{5,4},{6,5},{7,6},{8,7},{9,8},{10,9},{11,1... | collective-permute-start | bytes 24584 | tf_op jit(solution)/shard_map/ppermute | solution.py:21
  16.7 32.2 %collective-permute-start = (f32[128,4,512]{2,0,1:T(8,128)S(1)}, f32[128,4,512]{2,0,1:T(8,128)S(1)}, u32[]{:S(2)}, u32[]{:S(2)}) collective-permute-start(f32[128,4,512]{2,0,1:T(8,128)S(1)} %copy.34), channel_id=1, source_target_pairs={{0,1},{1,2},{2,3},{3,4},{4,5},{5,6},{6,7},{7,8},{8,9},{9,10},{10,1... | collective-permute-start | bytes 3145736 | tf_op jit(solution)/shard_map/ppermute | solution.py:20
  22.3 27.0 %collective-permute-start.1 = (f32[128,4,512]{2,0,1:T(8,128)}, f32[128,4,512]{2,0,1:T(8,128)}, u32[]{:S(2)}, u32[]{:S(2)}) collective-permute-start(f32[128,4,512]{2,0,1:T(8,128)} %copy.35), channel_id=1, source_target_pairs={{1,0},{2,1},{3,2},{4,3},{5,4},{6,5},{7,6},{8,7},{9,8},{10,9},{11,1... | collective-permute-start | bytes 3145736 | tf_op jit(solution)/shard_map/ppermute | solution.py:21
  23.6 25.2 %copy-start.24 = (f32[128]{0:T(128)}, f32[128]{0:T(128)S(1)}, u32[]{:S(2)}) copy-start(f32[128]{0:T(128)S(1)} %get-tuple-element.27) | copy-start | bytes 1540
  23.6 25.2 %copy-start.26 = (f32[128]{0:T(128)}, f32[128]{0:T(128)S(1)}, u32[]{:S(2)}) copy-start(f32[128]{0:T(128)S(1)} %get-tuple-element.28) | copy-start | bytes 1540
  23.6 25.2 %copy-start.28 = (f32[128]{0:T(128)}, f32[128]{0:T(128)S(1)}, u32[]{:S(2)}) copy-start(f32[128]{0:T(128)S(1)} %get-tuple-element.29) | copy-start | bytes 1540
  23.6 25.2 %copy-start.30 = (f32[128]{0:T(128)}, f32[128]{0:T(128)S(1)}, u32[]{:S(2)}) copy-start(f32[128]{0:T(128)S(1)} %get-tuple-element.30) | copy-start | bytes 1540
  23.6 25.2 %copy-start.32 = (f32[128]{0:T(128)}, f32[128]{0:T(128)S(1)}, u32[]{:S(2)}) copy-start(f32[128]{0:T(128)S(1)} %get-tuple-element.31) | copy-start | bytes 1540
  23.7 25.2 %copy-start.34 = (f32[128]{0:T(128)}, f32[128]{0:T(128)S(1)}, u32[]{:S(2)}) copy-start(f32[128]{0:T(128)S(1)} %get-tuple-element.32) | copy-start | bytes 1540
  23.7 25.2 %copy-start.36 = (f32[128]{0:T(128)}, f32[128]{0:T(128)S(1)}, u32[]{:S(2)}) copy-start(f32[128]{0:T(128)S(1)} %get-tuple-element.33) | copy-start | bytes 1540
  33.9 15.0 %copy-start.6 = (f32[24,512]{1,0:T(8,128)}, f32[24,512]{1,0:T(8,128)S(1)}, u32[]{:S(2)}) copy-start(f32[24,512]{1,0:T(8,128)S(1)} %get-tuple-element.22) | copy-start | bytes 147460
  33.9 15.0 %copy-start.8 = (f32[24,512]{1,0:T(8,128)}, f32[24,512]{1,0:T(8,128)S(1)}, u32[]{:S(2)}) copy-start(f32[24,512]{1,0:T(8,128)S(1)} %get-tuple-element.23) | copy-start | bytes 147460
  34.0 14.9 %copy-start.10 = (f32[24,512]{1,0:T(8,128)}, f32[24,512]{1,0:T(8,128)S(1)}, u32[]{:S(2)}) copy-start(f32[24,512]{1,0:T(8,128)S(1)} %get-tuple-element.16) | copy-start | bytes 147460
  34.0 14.9 %copy-start.12 = (f32[24,512]{1,0:T(8,128)}, f32[24,512]{1,0:T(8,128)S(1)}, u32[]{:S(2)}) copy-start(f32[24,512]{1,0:T(8,128)S(1)} %get-tuple-element.17) | copy-start | bytes 147460
  34.0 14.9 %copy-start.14 = (f32[24,512]{1,0:T(8,128)}, f32[24,512]{1,0:T(8,128)S(1)}, u32[]{:S(2)}) copy-start(f32[24,512]{1,0:T(8,128)S(1)} %get-tuple-element.18) | copy-start | bytes 147460
  34.0 14.9 %copy-start.16 = (f32[24,512]{1,0:T(8,128)}, f32[24,512]{1,0:T(8,128)S(1)}, u32[]{:S(2)}) copy-start(f32[24,512]{1,0:T(8,128)S(1)} %get-tuple-element.19) | copy-start | bytes 147460
  34.0 14.9 %copy-start.18 = (f32[24,512]{1,0:T(8,128)}, f32[24,512]{1,0:T(8,128)S(1)}, u32[]{:S(2)}) copy-start(f32[24,512]{1,0:T(8,128)S(1)} %get-tuple-element.20) | copy-start | bytes 147460
  34.0 14.9 %copy-start.20 = (f32[24,512]{1,0:T(8,128)}, f32[24,512]{1,0:T(8,128)S(1)}, u32[]{:S(2)}) copy-start(f32[24,512]{1,0:T(8,128)S(1)} %get-tuple-element.21) | copy-start | bytes 147460
  50.9 1.0 copy-start.3
  51.9 3.4 copy-start.2
  51.9 3.4 copy-start.7
  51.9 3.5 copy-start.9
  51.9 3.5 copy-start.11
  51.9 3.4 copy-start.13
  51.9 3.4 copy-start.15
  51.9 3.4 copy-start.17
  51.9 3.4 copy-start.19
  51.9 3.4 copy-start.21
  51.9 3.4 copy-start.25
  51.9 3.4 copy-start.27
  51.9 3.4 copy-start.29
  51.9 3.4 copy-start.31
  52.0 3.4 copy-start.33
  52.0 3.4 copy-start.35
  52.0 3.4 copy-start.37
  71.1 11.3 %copy-start.46 = (pred[20]{0:T(512)(128)(4,1)S(1)}, pred[20]{0:T(512)(128)(4,1)}, u32[]{:S(2)}) copy-start(pred[20]{0:T(512)(128)(4,1)} %compare_and_fusion.1) | copy-start | bytes 64
  82.4 16.6 %copy-start = (f32[128,22,512]{0,2,1:T(8,128)}, f32[128,22,512]{0,2,1:T(8,128)S(1)}, u32[]{:S(2)}) copy-start(f32[128,22,512]{0,2,1:T(8,128)S(1)} %get-tuple-element.11) | copy-start | bytes 17301508
  82.4 16.7 %copy-start.45 = (pred[18]{0:T(512)(128)(4,1)S(1)}, pred[18]{0:T(512)(128)(4,1)}, u32[]{:S(2)}) copy-start(pred[18]{0:T(512)(128)(4,1)} %compare_and_fusion.2) | copy-start | bytes 58
  99.0 10.9 %copy-start.1 = (f32[128,20,512]{0,2,1:T(8,128)}, f32[128,20,512]{0,2,1:T(8,128)S(1)}, u32[]{:S(2)}) copy-start(f32[128,20,512]{0,2,1:T(8,128)S(1)} %get-tuple-element.9) | copy-start | bytes 15728644
  99.0 10.9 %copy-start.40 = (pred[128]{0:T(512)(128)(4,1)S(1)}, pred[128]{0:T(512)(128)(4,1)}, u32[]{:S(2)}) copy-start(pred[128]{0:T(512)(128)(4,1)} %get-tuple-element.4) | copy-start | bytes 388
  99.0 10.9 %copy-start.41 = (pred[128]{0:T(512)(128)(4,1)S(1)}, pred[128]{0:T(512)(128)(4,1)}, u32[]{:S(2)}) copy-start(pred[128]{0:T(512)(128)(4,1)} %get-tuple-element.34) | copy-start | bytes 388
  99.0 10.9 %copy-start.42 = (pred[128]{0:T(512)(128)(4,1)S(1)}, pred[128]{0:T(512)(128)(4,1)}, u32[]{:S(2)}) copy-start(pred[128]{0:T(512)(128)(4,1)} %get-tuple-element.35) | copy-start | bytes 388
  99.1 10.9 %copy-start.43 = (pred[128]{0:T(512)(128)(4,1)S(1)}, pred[128]{0:T(512)(128)(4,1)}, u32[]{:S(2)}) copy-start(pred[128]{0:T(512)(128)(4,1)} %get-tuple-element.36) | copy-start | bytes 388
  99.1 10.9 %copy-start.44 = (pred[16]{0:T(512)(128)(4,1)S(1)}, pred[16]{0:T(512)(128)(4,1)}, u32[]{:S(2)}) copy-start(pred[16]{0:T(512)(128)(4,1)} %compare_and_fusion.3) | copy-start | bytes 52
  137.3 5.9 %copy-start.38 = (s32[512]{0:T(512)S(1)}, s32[512]{0:T(512)}, u32[]{:S(2)}) copy-start(s32[512]{0:T(512)} %param.12) | copy-start | bytes 6148
  137.3 6.1 %copy-start.5 = (f32[69,2048]{1,0:T(8,128)S(1)}, f32[69,2048]{1,0:T(8,128)}, u32[]{:S(2)}) copy-start(f32[69,2048]{1,0:T(8,128)} %param.13) | copy-start | bytes 1695748
  137.3 6.1 %copy-start.39 = (f32[512]{0:T(512)S(1)}, f32[512]{0:T(512)}, u32[]{:S(2)}) copy-start(f32[512]{0:T(512)} %param.11) | copy-start | bytes 6148
  137.3 53.4 %all-to-all-start = ((f32[2,2,128,2048]{3,2,1,0:T(8,128)}), f32[2,2,128,2048]{3,2,1,0:T(8,128)}, u32[]{:S(2)}, u32[]{:S(2)}) async-start(f32[2,2,128,2048]{3,2,1,0:T(8,128)} %bitcast.31), calls=%async_computation | async-start | bytes 8388608 | tf_op jit(solution)/shard_map/all_to_all | solution.py:42
  143.0 234.9 %all-reduce.10.cloned.1.call-start = ((), (), s32[]{:S(2)}) async-start(), calls=%async_computation.2 | async-start | bytes 8388608 | tf_op jit(solution)/shard_map/psum | solution.py:136
  190.6 12.4 %slice-start = ((s8[8388608]{0:T(1024)(128)(4,1)}), s8[4194304]{0:T(1024)(128)(4,1)S(1)}, s32[]{:S(2)}) async-start(s8[8388608]{0:T(1024)(128)(4,1)} %bitcast.34), calls=%async_computation.3 | async-start | bytes 8388608
  193.2 9.8 %slice-start.1 = ((s8[8388608]{0:T(1024)(128)(4,1)}), s8[4194304]{0:T(1024)(128)(4,1)S(1)}, s32[]{:S(2)}) async-start(s8[8388608]{0:T(1024)(128)(4,1)} %bitcast.34), calls=%async_computation.4 | async-start | bytes 8388608
  202.5 2.2 copy-start.4
  202.5 2.2 copy-start.23
  210.7 2.1 copy-start.47
Sparse Core Ops, SparseCore 0:
  219.1 158.7 all-reduce.9
where the time goes:
time: 394 us; the launch traced here: 393 us
  waiting for transfers between devices  186 us (47%)
  other arithmetic  99.4 us (25%)
  matrix products  40.2 us (10%)
  local copies, waits for them, and re-layouts  26.5 us (7%)
  starting transfers between devices  17 us (4%)
  between operations  14.8 us (4%)
  blocking collectives  9.24 us (2%)
    psum x1, waiting for transfers between devices, on_device(): back = lax.psum(partial_back, GRP_TILE)  144 us
    div x4, other arithmetic, advance(): spread = kappa * (1.0 + steep * ratio) / (1.0 + ratio)  54.4 us
    all_to_all x1, waiting for transfers between devices, turned_blocks(): out = lax.all_to_all(out, axes[k], k, k, tiled=True)  42.2 us
    select_n x1, other arithmetic, on_device(): jnp.where(pick_here == step + 1, wide[:, margin:margin + rows], snapshot)  21.7 us
    add x1, other arithmetic, coefficients(): kappa = kappa + picked[None] * table[:, klass][:, None, None]  14.8 us
    dot_general x1, matrix products, on_device(): lax.dot_general(hidden, slope, (((0,), (0,)), ((), ())), preferred_elemen...  14.6 us
    unnamed x103, local copies, waits for them, and re-layouts  12.4 us
    all_to_all x1, blocking collectives, turned_blocks(): out = lax.all_to_all(out, axes[k], k, k, tiled=True)  9.24 us
  transfers between devices with their start and end apart: 6, of which 2 were waited for; matrix products, arithmetic and copies ran while one was open for 13% of the time, Pallas kernels for 0%

commit v1 on v0

--- a/solution.py
+++ b/solution.py
@@ -133,7 +133,7 @@
     partial_back = lax.dot_general(
         slope, output_layer, (((1,), (1,)), ((), ())), preferred_element_type=jnp.float32
     )
-    back = lax.psum(partial_back, GRP_TILE)
+    back = lax.psum(lax.psum(partial_back, "grp_0"), ("grp_1", "tile"))
     grad_in = lax.dot_general(
         feats, back * gain_slope, (((0,), (0,)), ((), ())), precision=lax.Precision.HIGHEST
     )

time: 394 us -> 969 us (2.46); the launches traced: 393 us -> 952 us
  waiting for transfers between devices: 186 us -> 745 us
    psum x1 -> x2, waiting for transfers between devices: 144 us -> 702 us  [on_device(): back = lax.psum(lax.psum(partial_back, 'grp_0'), ('grp_1', 'tile'))]
  transfers between devices with their start and end apart: 6 -> 7, of which waited for: 2 -> 3; matrix products, arithmetic and copies ran while one was open for 13% -> 5% of each run, Pallas kernels for 0% -> 0%
where the time goes in v1:
time: 969 us; the launch traced here: 952 us
  waiting for transfers between devices  745 us (77%)
  other arithmetic  99.4 us (10%)
  matrix products  40.1 us (4%)
  local copies, waits for them, and re-layouts  26.4 us (3%)
  starting transfers between devices  17.3 us (2%)
  between operations  14.8 us (2%)
    psum x2, waiting for transfers between devices, on_device(): back = lax.psum(lax.psum(partial_back, 'grp_0'), ('grp_1', 'tile'))  702 us
    div x4, other arithmetic, advance(): spread = kappa * (1.0 + steep * ratio) / (1.0 + ratio)  54.4 us
    all_to_all x1, waiting for transfers between devices, turned_blocks(): out = lax.all_to_all(out, axes[k], k, k, tiled=True)  42.2 us
    select_n x1, other arithmetic, on_device(): jnp.where(pick_here == step + 1, wide[:, margin:margin + rows], snapshot)  21.7 us
  transfers between devices with their start and end apart: 7, of which 3 were waited for; matrix products, arithmetic and copies ran while one was open for 5% of the time, Pallas kernels for 0%

profile of v1, /device:TPU:1, one launch (start us, length us, event | category | flops | bytes accessed | tf_op | source)
XLA Modules:
  0.0 951.9 jit_solution(806825170667194145)
XLA Ops:
  7.2 0.0 copy-start.22
  7.2 0.8 broadcast_add_fusion
  8.0 4.4 collective-permute-start.2
  12.3 1.3 collective-permute-start.3
  13.6 2.7 fusion.96
  16.4 0.3 copy.34
  16.7 4.2 collective-permute-start
  21.0 1.3 copy.35
  22.3 1.3 collective-permute-start.1
  23.6 0.0 copy-start.24
  23.7 0.6 compare_and_fusion.3
  24.3 0.6 compare_and_fusion
  24.8 0.6 compare_and_fusion.1
  25.4 1.3 broadcast_compare_fusion.3
  26.7 0.6 broadcast_compare_fusion.2
  27.3 0.6 compare_and_fusion.2
  27.8 5.3 copy.29
  33.1 0.8 dynamic_slice.11
  33.9 0.0 collective-permute-done.2
  33.9 0.0 collective-permute-done.3
  33.9 0.0 copy-start.8
  34.0 0.0 copy-start.10
  34.0 0.0 copy-start.12
  34.0 0.0 copy-start.14
  34.0 0.0 copy-start.16
  34.0 14.8 %multiply_add_fusion = f32[128,24,512]{0,2,1:T(8,128)} fusion(f32[128]{0:T(128)S(1)} %get-tuple-element.27, f32[24,512]{1,0:T(8,128)S(1)} %get-tuple-element.23, f32[128]{0:T(128)S(1)} %get-tuple-element.28, f32[24,512]{1,0:T(8,128)S(1)} %get-tuple-element.22, f32[128]{0:T(128)S(1)} %get-tuple-element.29, f32[24,512]{1,0:T(8,128)S(1)} %get-tuple-element.21, ...), kind=kLoop, calls=%fused_computation.3 | loop fusion | flops 23592960 | bytes 6688768 | tf_op jit(solution)/shard_map/add | solution.py:57
  49.0 0.0 collective-permute-done
  49.0 0.3 copy.28
  49.3 0.0 collective-permute-done.1
  49.3 1.5 copy.30
  50.9 0.0 copy-start.3
  50.9 1.0 copy-done.3
  51.9 0.0 copy-start.25
  52.0 2.7 pad_maximum_fusion
  54.7 0.6 copy-done.2
  55.4 15.7 %add_divide_fusion = f32[128,24,512]{0,2,1:T(8,128)S(1)} fusion(f32[128]{0:T(128)S(1)} %dynamic_slice.11, f32[128,4,512]{0,2,1:T(8,128)} %copy-done.3, f32[128,16,512]{0,2,1:T(8,128)S(1)} %copy-done.2, f32[128,4,512]{0,2,1:T(8,128)S(1)} %copy.28, f32[128]{0:T(128)S(1)} %copy-done.25, f32[24,512]{1,0:T(8,128)S(1)} %copy-done.9, f32[128]{0:T(128)S(1)} %copy-done.27, ...), kind=kLoop, calls=%fused_computation.2 | loop fusion | flops 36175872 | bytes 12980736 | tf_op jit(solution)/shard_map/div | solution.py:63
  71.1 11.3 %fusion.11 = (f32[128,22,512]{0,2,1:T(8,128)}, f32[128,22,512]{0,2,1:T(8,128)S(1)}) fusion(f32[128,24,512]{0,2,1:T(8,128)} %multiply_add_fusion, f32[128]{0:T(128)S(1)} %dynamic_slice.11, f32[128,24,512]{0,2,1:T(8,128)S(1)} %pad_maximum_fusion, f32[128,24,512]{0,2,1:T(8,128)S(1)} %add_divide_fusion, pred[22]{0:T(512)(128)(4,1)} %compare_and_fusion), kind=kLoop, calls=%fused_computation.20 | loop fusion | flops 38928384 | bytes 64487960 | tf_op jit(solution)/shard_map/div | solution.py:63
  82.4 16.6 %fusion.29 = (f32[128,20,512]{0,2,1:T(8,128)S(1)}, f32[128,20,512]{0,2,1:T(8,128)S(1)}) fusion(f32[128,24,512]{0,2,1:T(8,128)} %multiply_add_fusion, f32[128]{0:T(128)S(1)} %dynamic_slice.11, f32[128,22,512]{0,2,1:T(8,128)S(1)} %get-tuple-element.11, f32[128,22,512]{0,2,1:T(8,128)} %get-tuple-element.10, pred[20]{0:T(512)(128)(4,1)S(1)} %copy-done.46), kind=kLoop, calls=%fused_computation.47 | loop fusion | flops 35389440 | bytes 58721280 | tf_op jit(solution)/shard_map/div | solution.py:63
  99.1 10.9 %fusion.47 = (f32[128,18,512]{0,2,1:T(8,128)}, f32[128,18,512]{0,2,1:T(8,128)}) fusion(f32[128,24,512]{0,2,1:T(8,128)} %multiply_add_fusion, f32[128]{0:T(128)S(1)} %dynamic_slice.11, f32[128,20,512]{0,2,1:T(8,128)S(1)} %get-tuple-element.9, f32[128,20,512]{0,2,1:T(8,128)S(1)} %get-tuple-element.8, pred[18]{0:T(512)(128)(4,1)S(1)} %copy-done.45), kind=kLoop, calls=%fused_computation.74 | loop fusion | flops 31850496 | bytes 52954112 | tf_op jit(solution)/shard_map/div | solution.py:63
  110.0 21.7 %fusion.60 = f32[128,16,512]{0,2,1:T(8,128)} fusion(f32[128,18,512]{0,2,1:T(8,128)} %get-tuple-element.6, f32[128,18,512]{0,2,1:T(8,128)} %get-tuple-element.7, f32[128,22,512]{0,2,1:T(8,128)} %copy-done, f32[128,20,512]{0,2,1:T(8,128)} %copy-done.1, pred[16]{0:T(512)(128)(4,1)S(1)} %copy-done.44, pred[128]{0:T(512)(128)(4,1)S(1)} %copy-done.43, ...), kind=kLoop, calls=%fused_computation.95 | loop fusion | flops 26214400 | bytes 47186448 | tf_op jit(solution)/shard_map/jit(_where)/select_n | solution.py:114
  131.7 5.6 copy.31
  137.3 5.8 all-to-all-start
  143.0 0.0 all-reduce.11.cloned.1.call-start
  143.1 0.1 eq.141
  143.2 0.1 compare_convert_fusion
  143.3 0.1 fusion.87
  143.4 5.1 fusion.88
  148.5 42.2 %all-to-all-done = f32[2,2,128,2048]{3,2,1,0:T(8,128)} async-done(((f32[2,2,128,2048]{3,2,1,0:T(8,128)}), f32[2,2,128,2048]{3,2,1,0:T(8,128)}, u32[]{:S(2)}, u32[]{:S(2)}) %all-to-all-start) | async-done | bytes 4194336 | tf_op jit(solution)/shard_map/all_to_all | solution.py:42
  190.6 2.6 copy.32
  193.2 0.0 slice-start.1
  193.3 9.2 all_to_all.10
  202.5 0.5 copy.33
  203.0 1.7 copy-done.4
  204.7 6.1 convert_reduce_fusion
  210.7 1.9 copy-done.47
  212.7 6.1 fusion.92
  218.8 0.0 all-reduce.11.cloned.1.call-update
  218.8 0.3 all-reduce.13.cloned.1.call-start
  219.1 120.4 %all-reduce.11.cloned.1.call-done = f32[512,2048]{1,0:T(8,128)} async-done(((f32[512,2048]{1,0:T(8,128)}), f32[512,2048]{1,0:T(8,128)}) %all-reduce.11.cloned.1.call-update) | async-done | bytes 4194320 | tf_op jit(solution)/shard_map/psum | solution.py:136
  339.5 0.0 all-reduce.13.cloned.1.call-update
  339.5 0.6 multiply_subtract_fusion
  340.1 14.6 %subtract_convert_fusion = bf16[2048,2048]{1,0:T(8,128)(2,1)} fusion(bf16[2048,2048]{1,0:T(8,128)(2,1)} %param.14, f32[512,2048]{1,0:T(8,128)} %copy-done.47, f32[512,2048]{1,0:T(8,128)} %fusion.88), kind=kOutput, calls=%fused_computation | convolution fusion | flops 4319084544 | bytes 25165824 | tf_op jit(solution)/shard_map/dot_general | solution.py:127
  354.7 582.1 %all-reduce.13.cloned.1.call-done = f32[512,2048]{1,0:T(8,128)} async-done(((f32[512,2048]{1,0:T(8,128)}), f32[512,2048]{1,0:T(8,128)}) %all-reduce.13.cloned.1.call-update) | async-done | bytes 4194320 | tf_op jit(solution)/shard_map/psum | solution.py:136
  936.8 8.2 fusion.83
  (94 shorter events, 0.3 us)
Async XLA Ops:
  7.2 16.4 %copy-start.22 = (s32[512,8]{0,1:T(8,128)S(1)}, s32[512,8]{0,1:T(8,128)}, u32[]{:S(2)}) copy-start(s32[512,8]{0,1:T(8,128)} %param.10) | copy-start | bytes 49156
  8.0 25.9 %collective-permute-start.2 = (s32[4,512]{1,0:T(4,128)S(1)}, s32[4,512]{1,0:T(4,128)S(1)}, u32[]{:S(2)}, u32[]{:S(2)}) collective-permute-start(s32[4,512]{1,0:T(4,128)S(1)} %get-tuple-element.24), channel_id=1, source_target_pairs={{0,1},{1,2},{2,3},{3,4},{4,5},{5,6},{6,7},{7,8},{8,9},{9,10},{10,1... | collective-permute-start | bytes 24584 | tf_op jit(solution)/shard_map/ppermute | solution.py:20
  12.3 21.6 %collective-permute-start.3 = (s32[4,512]{1,0:T(4,128)S(1)}, s32[4,512]{1,0:T(4,128)S(1)}, u32[]{:S(2)}, u32[]{:S(2)}) collective-permute-start(s32[4,512]{1,0:T(4,128)S(1)} %get-tuple-element.25), channel_id=1, source_target_pairs={{1,0},{2,1},{3,2},{4,3},{5,4},{6,5},{7,6},{8,7},{9,8},{10,9},{11,1... | collective-permute-start | bytes 24584 | tf_op jit(solution)/shard_map/ppermute | solution.py:21
  16.7 32.2 %collective-permute-start = (f32[128,4,512]{2,0,1:T(8,128)S(1)}, f32[128,4,512]{2,0,1:T(8,128)S(1)}, u32[]{:S(2)}, u32[]{:S(2)}) collective-permute-start(f32[128,4,512]{2,0,1:T(8,128)S(1)} %copy.34), channel_id=1, source_target_pairs={{0,1},{1,2},{2,3},{3,4},{4,5},{5,6},{6,7},{7,8},{8,9},{9,10},{10,1... | collective-permute-start | bytes 3145736 | tf_op jit(solution)/shard_map/ppermute | solution.py:20
  22.3 27.0 %collective-permute-start.1 = (f32[128,4,512]{2,0,1:T(8,128)}, f32[128,4,512]{2,0,1:T(8,128)}, u32[]{:S(2)}, u32[]{:S(2)}) collective-permute-start(f32[128,4,512]{2,0,1:T(8,128)} %copy.35), channel_id=1, source_target_pairs={{1,0},{2,1},{3,2},{4,3},{5,4},{6,5},{7,6},{8,7},{9,8},{10,9},{11,1... | collective-permute-start | bytes 3145736 | tf_op jit(solution)/shard_map/ppermute | solution.py:21
  23.6 25.2 %copy-start.24 = (f32[128]{0:T(128)}, f32[128]{0:T(128)S(1)}, u32[]{:S(2)}) copy-start(f32[128]{0:T(128)S(1)} %get-tuple-element.27) | copy-start | bytes 1540
  23.6 25.2 %copy-start.26 = (f32[128]{0:T(128)}, f32[128]{0:T(128)S(1)}, u32[]{:S(2)}) copy-start(f32[128]{0:T(128)S(1)} %get-tuple-element.28) | copy-start | bytes 1540
  23.6 25.2 %copy-start.28 = (f32[128]{0:T(128)}, f32[128]{0:T(128)S(1)}, u32[]{:S(2)}) copy-start(f32[128]{0:T(128)S(1)} %get-tuple-element.29) | copy-start | bytes 1540
  23.6 25.2 %copy-start.30 = (f32[128]{0:T(128)}, f32[128]{0:T(128)S(1)}, u32[]{:S(2)}) copy-start(f32[128]{0:T(128)S(1)} %get-tuple-element.30) | copy-start | bytes 1540
  23.6 25.2 %copy-start.32 = (f32[128]{0:T(128)}, f32[128]{0:T(128)S(1)}, u32[]{:S(2)}) copy-start(f32[128]{0:T(128)S(1)} %get-tuple-element.31) | copy-start | bytes 1540
  23.7 25.2 %copy-start.34 = (f32[128]{0:T(128)}, f32[128]{0:T(128)S(1)}, u32[]{:S(2)}) copy-start(f32[128]{0:T(128)S(1)} %get-tuple-element.32) | copy-start | bytes 1540
  23.7 25.2 %copy-start.36 = (f32[128]{0:T(128)}, f32[128]{0:T(128)S(1)}, u32[]{:S(2)}) copy-start(f32[128]{0:T(128)S(1)} %get-tuple-element.33) | copy-start | bytes 1540
  33.9 15.0 %copy-start.6 = (f32[24,512]{1,0:T(8,128)}, f32[24,512]{1,0:T(8,128)S(1)}, u32[]{:S(2)}) copy-start(f32[24,512]{1,0:T(8,128)S(1)} %get-tuple-element.22) | copy-start | bytes 147460
  33.9 15.0 %copy-start.8 = (f32[24,512]{1,0:T(8,128)}, f32[24,512]{1,0:T(8,128)S(1)}, u32[]{:S(2)}) copy-start(f32[24,512]{1,0:T(8,128)S(1)} %get-tuple-element.23) | copy-start | bytes 147460
  34.0 14.9 %copy-start.10 = (f32[24,512]{1,0:T(8,128)}, f32[24,512]{1,0:T(8,128)S(1)}, u32[]{:S(2)}) copy-start(f32[24,512]{1,0:T(8,128)S(1)} %get-tuple-element.16) | copy-start | bytes 147460
  34.0 14.9 %copy-start.12 = (f32[24,512]{1,0:T(8,128)}, f32[24,512]{1,0:T(8,128)S(1)}, u32[]{:S(2)}) copy-start(f32[24,512]{1,0:T(8,128)S(1)} %get-tuple-element.17) | copy-start | bytes 147460
  34.0 14.9 %copy-start.14 = (f32[24,512]{1,0:T(8,128)}, f32[24,512]{1,0:T(8,128)S(1)}, u32[]{:S(2)}) copy-start(f32[24,512]{1,0:T(8,128)S(1)} %get-tuple-element.18) | copy-start | bytes 147460
  34.0 14.9 %copy-start.16 = (f32[24,512]{1,0:T(8,128)}, f32[24,512]{1,0:T(8,128)S(1)}, u32[]{:S(2)}) copy-start(f32[24,512]{1,0:T(8,128)S(1)} %get-tuple-element.19) | copy-start | bytes 147460
  34.0 14.9 %copy-start.18 = (f32[24,512]{1,0:T(8,128)}, f32[24,512]{1,0:T(8,128)S(1)}, u32[]{:S(2)}) copy-start(f32[24,512]{1,0:T(8,128)S(1)} %get-tuple-element.20) | copy-start | bytes 147460
  34.0 14.9 %copy-start.20 = (f32[24,512]{1,0:T(8,128)}, f32[24,512]{1,0:T(8,128)S(1)}, u32[]{:S(2)}) copy-start(f32[24,512]{1,0:T(8,128)S(1)} %get-tuple-element.21) | copy-start | bytes 147460
  50.9 1.0 copy-start.3
  51.9 3.4 copy-start.2
  51.9 3.4 copy-start.7
  51.9 3.5 copy-start.9
  51.9 3.5 copy-start.11
  51.9 3.4 copy-start.13
  51.9 3.4 copy-start.15
  51.9 3.4 copy-start.17
  51.9 3.4 copy-start.19
  51.9 3.4 copy-start.21
  51.9 3.4 copy-start.25
  51.9 3.4 copy-start.27
  51.9 3.4 copy-start.29
  51.9 3.4 copy-start.31
  52.0 3.4 copy-start.33
  52.0 3.4 copy-start.35
  52.0 3.4 copy-start.37
  71.1 11.3 %copy-start.46 = (pred[20]{0:T(512)(128)(4,1)S(1)}, pred[20]{0:T(512)(128)(4,1)}, u32[]{:S(2)}) copy-start(pred[20]{0:T(512)(128)(4,1)} %compare_and_fusion.1) | copy-start | bytes 64
  82.4 16.6 %copy-start = (f32[128,22,512]{0,2,1:T(8,128)}, f32[128,22,512]{0,2,1:T(8,128)S(1)}, u32[]{:S(2)}) copy-start(f32[128,22,512]{0,2,1:T(8,128)S(1)} %get-tuple-element.11) | copy-start | bytes 17301508
  82.4 16.7 %copy-start.45 = (pred[18]{0:T(512)(128)(4,1)S(1)}, pred[18]{0:T(512)(128)(4,1)}, u32[]{:S(2)}) copy-start(pred[18]{0:T(512)(128)(4,1)} %compare_and_fusion.2) | copy-start | bytes 58
  99.0 10.9 %copy-start.1 = (f32[128,20,512]{0,2,1:T(8,128)}, f32[128,20,512]{0,2,1:T(8,128)S(1)}, u32[]{:S(2)}) copy-start(f32[128,20,512]{0,2,1:T(8,128)S(1)} %get-tuple-element.9) | copy-start | bytes 15728644
  99.0 10.9 %copy-start.40 = (pred[128]{0:T(512)(128)(4,1)S(1)}, pred[128]{0:T(512)(128)(4,1)}, u32[]{:S(2)}) copy-start(pred[128]{0:T(512)(128)(4,1)} %get-tuple-element.4) | copy-start | bytes 388
  99.0 10.9 %copy-start.41 = (pred[128]{0:T(512)(128)(4,1)S(1)}, pred[128]{0:T(512)(128)(4,1)}, u32[]{:S(2)}) copy-start(pred[128]{0:T(512)(128)(4,1)} %get-tuple-element.34) | copy-start | bytes 388
  99.0 10.9 %copy-start.42 = (pred[128]{0:T(512)(128)(4,1)S(1)}, pred[128]{0:T(512)(128)(4,1)}, u32[]{:S(2)}) copy-start(pred[128]{0:T(512)(128)(4,1)} %get-tuple-element.35) | copy-start | bytes 388
  99.1 10.9 %copy-start.43 = (pred[128]{0:T(512)(128)(4,1)S(1)}, pred[128]{0:T(512)(128)(4,1)}, u32[]{:S(2)}) copy-start(pred[128]{0:T(512)(128)(4,1)} %get-tuple-element.36) | copy-start | bytes 388
  99.1 10.9 %copy-start.44 = (pred[16]{0:T(512)(128)(4,1)S(1)}, pred[16]{0:T(512)(128)(4,1)}, u32[]{:S(2)}) copy-start(pred[16]{0:T(512)(128)(4,1)} %compare_and_fusion.3) | copy-start | bytes 52
  137.3 5.9 copy-start.38
  137.3 6.1 copy-start.5
  137.3 6.1 copy-start.39
  137.3 53.4 %all-to-all-start = ((f32[2,2,128,2048]{3,2,1,0:T(8,128)}), f32[2,2,128,2048]{3,2,1,0:T(8,128)}, u32[]{:S(2)}, u32[]{:S(2)}) async-start(f32[2,2,128,2048]{3,2,1,0:T(8,128)} %bitcast.31), calls=%async_computation | async-start | bytes 8388608 | tf_op jit(solution)/shard_map/all_to_all | solution.py:42
  143.0 196.4 %all-reduce.11.cloned.1.call-start = ((), (), s32[]{:S(2)}) async-start(), calls=%async_computation.2 | async-start | bytes 8388608 | tf_op jit(solution)/shard_map/psum | solution.py:136
  190.6 12.4 %slice-start = ((s8[8388608]{0:T(1024)(128)(4,1)}), s8[4194304]{0:T(1024)(128)(4,1)S(1)}, s32[]{:S(2)}) async-start(s8[8388608]{0:T(1024)(128)(4,1)} %bitcast.34), calls=%async_computation.4 | async-start | bytes 8388608
  193.2 9.8 %slice-start.1 = ((s8[8388608]{0:T(1024)(128)(4,1)}), s8[4194304]{0:T(1024)(128)(4,1)S(1)}, s32[]{:S(2)}) async-start(s8[8388608]{0:T(1024)(128)(4,1)} %bitcast.34), calls=%async_computation.5 | async-start | bytes 8388608
  202.5 2.2 copy-start.4
  202.5 2.2 copy-start.23
  210.7 1.9 copy-start.47
  218.8 718.0 %all-reduce.13.cloned.1.call-start = ((), (), s32[]{:S(2)}) async-start(), calls=%async_computation.3 | async-start | bytes 8388608 | tf_op jit(solution)/shard_map/psum | solution.py:136
Sparse Core Ops, SparseCore 0:
  218.9 120.4 all-reduce.10
  342.1 594.6 all-reduce.12
